TPU v7x, 256 devices: a whole 4x4x8 slice. The times are simulated.
256 devices in a mesh: region: 4 (over x), member: 64 (over z, y, core).
Axes of the slice: x: 4, y: 4, z: 8, core: 2. Of those that a mesh axis runs over, the one named last changes fastest.
Arguments:
- right_side: float32 [3, 262144], P(None, ('region', 'member')), may hold values from -6 to 6
- fine_blocks: float32 [27, 3, 3, 262144], P(None, None, None, ('region', 'member')), as said below
- fine_links: int32 [26, 262144], P(None, ('region', 'member')), may hold values from 0 to 1279, as said below
- coarse_blocks: float32 [27, 3, 3, 32768], P(None, None, None, ('region', 'member')), as said below
- coarse_links: int32 [26, 32768], P(None, ('region', 'member')), may hold values from 0 to 255, as said below
Outputs:
- correction: float32 [3, 262144], P(None, ('region', 'member'))
- final_residual: float32 [3, 262144], P(None, ('region', 'member'))
Inputs may be any that keep to these rules, and one draw needn't show every extreme that they name: `fine_links`: A code of 1024 or more occurs only for one of the first 64 blocks of a device, and only toward a device that exists: the device before or after it in the same region, or the device with the same member index in the region before or after. `coarse_links`: as for fine_links, with 128 coarse nodes a device and 32 in place of 64. `fine_blocks`: each node's diagonal block is strictly dominant: in each row the diagonal entry exceeds 1.1 times the sum of magnitudes of that row's other entries over all 27 blocks. `coarse_blocks`: diagonally dominant as fine_blocks.
All inputs are finite; a program needn't handle non-finite values.
Results may differ from a plain program's by a relative error of at most 0.0003.
Values sent between devices are 32-bit elements; how exact they have to be, the bound alone decides.
A program may use at most 128 MiB of HBM per device.

v0:
```python
import jax
import jax.numpy as jnp
from jax import lax
from jax.sharding import PartitionSpec as P

STEPS = 3


relax = 0.6


def extended_2(shard, sides, width):
    for axis, dim in sides:
        peers, length = (lax.axis_size(axis), shard.shape[dim])
        up = [(i, (i + 1) % peers) for i in range(peers - 1)]
        down = [(j, i) for i, j in up]
        last = lax.slice_in_dim(shard, length - width, length, axis=dim)
        leading = lax.slice_in_dim(shard, 0, width, axis=dim)
        before = lax.ppermute(last, axis, up)
        after = lax.ppermute(leading, axis, down)
        shard = jnp.concatenate([before, shard, after], axis=dim)
    return shard


def invert(block):
    a, b, c = (block[0, 0], block[0, 1], block[0, 2])
    d, e, f = (block[1, 0], block[1, 1], block[1, 2])
    g, h, i = (block[2, 0], block[2, 1], block[2, 2])
    co_a = e * i - f * h
    co_b = f * g - d * i
    co_c = d * h - e * g
    det = a * co_a + b * co_b + c * co_c
    rows = [
        [co_a, c * h - b * i, b * f - c * e],
        [co_b, a * i - c * g, c * d - a * f],
        [co_c, b * g - a * h, a * e - b * d],
    ]
    return jnp.stack([jnp.stack(row) for row in rows]) / det


def blockmul(matrix, vector):
    return jnp.sum(matrix * vector[None], axis=1)


def fetch(field, face, coarse):
    count = field.shape[1]
    source = field[None, None]
    if coarse:
        beside_all = extended_2(source, (("region", 0), ("member", 1)), 1)
    else:
        beside_all = extended_2(source, (("region", 0), ("member", 1)), 1)
    left = beside_all[1, 0, :, count - face :]
    right = beside_all[1, 2, :, :face]
    lower = beside_all[0, 1, :, :face]
    upper = beside_all[2, 1, :, :face]
    return jnp.concatenate([field, left, right, lower, upper], axis=1)


def apply_index(blocks, index, field, extended):
    values = jnp.transpose(jnp.take(extended, index, axis=1), (1, 0, 2))
    return blockmul(blocks[26], field) + jnp.sum(blocks[:26] * values[:, None, :, :], axis=(0, 2))


def operate(blocks, index, field, face, coarse):
    return apply_index(blocks, index, field, fetch(field, face, coarse))


def body(right_side, fine_blocks, fine_links, coarse_blocks, coarse_links):
    fine_face = right_side.shape[1] // 16
    coarse_dev = coarse_blocks.shape[3]
    coarse_face = coarse_dev // 4
    inverse_fine = invert(fine_blocks[26])
    first = relax * blockmul(inverse_fine, right_side)
    first_res = right_side - operate(fine_blocks, fine_links, first, fine_face, False)
    smoothed = first + relax * blockmul(inverse_fine, first_res)
    smooth_res = right_side - operate(fine_blocks, fine_links, smoothed, fine_face, False)
    coarse_rhs = jnp.sum(smooth_res.reshape(3, -1, 8), axis=2)

    def coarse_op(field):
        return operate(coarse_blocks, coarse_links, field, coarse_face, True)

    resid = coarse_rhs
    direction = coarse_rhs
    error = jnp.zeros_like(coarse_rhs)
    rho = lax.psum(jnp.sum(resid * resid), ("region", "member"))
    for step in range(STEPS):
        image = coarse_op(direction)
        alpha = rho / lax.psum(jnp.sum(coarse_rhs * image), ("region", "member"))
        middle = resid - alpha * image
        second = coarse_op(middle)
        cross, square = lax.psum(
            (jnp.sum(second * middle), jnp.sum(second * second)), ("region", "member")
        )
        omega = cross / square
        error = error + alpha * direction + omega * middle
        resid = middle - omega * second
        if step + 1 < STEPS:
            rho_new = lax.psum(jnp.sum(coarse_rhs * resid), ("region", "member"))
        if step + 1 < STEPS:
            beta = rho_new / rho * (alpha / omega)
            direction = resid + beta * (direction - omega * image)
            rho = rho_new
    lifted = smoothed + jnp.repeat(error, 8, axis=1)
    lifted_res = right_side - operate(fine_blocks, fine_links, lifted, fine_face, False)
    correction = lifted + relax * blockmul(inverse_fine, lifted_res)
    final_residual = right_side - operate(fine_blocks, fine_links, correction, fine_face, False)
    return (correction, final_residual)


def solution(mesh):
    return jax.shard_map(
        body,
        mesh=mesh,
        in_specs=(
            P(None, ("region", "member")),
            P(None, None, None, ("region", "member")),
            P(None, ("region", "member")),
            P(None, None, None, ("region", "member")),
            P(None, ("region", "member")),
        ),
        out_specs=(P(None, ("region", "member")), P(None, ("region", "member"))),
        check_vma=False,
    )
```

profile of v0, /device:TPU:1, one launch (start us, length us, event | category | flops | bytes accessed | tf_op | source)
XLA Modules:
  0.0 1287.2 jit_solution(18172876742450923870)
XLA Ops:
  2.6 3.9 collective-permute-start
  15.7 3.1 collective-permute-start.2
  20.3 88.1 %gather_fusion = f32[26624,3]{1,0:T(8,128)} fusion(f32[3,1280]{0,1:T(8,128)S(1)} %copy.237, s32[26624]{0:T(1024)S(1)} %broadcast_clamp_fusion), kind=kCustom, calls=%fused_computation.clone | custom fusion | bytes 745472 | tf_op jit(solution)/shard_map/jit(_take)/gather | solution.py:60
  108.3 10.3 select_bitcast_fusion.3
  118.7 9.5 copy.238
  128.4 4.3 collective-permute-start.4
  134.2 3.2 collective-permute-done.5
  139.7 5.1 collective-permute-start.6
  146.3 88.1 %gather_fusion.1 = f32[26624,3]{1,0:T(8,128)} fusion(f32[3,1280]{0,1:T(8,128)S(1)} %copy.242, s32[26624]{0:T(1024)S(1)} %broadcast_clamp_fusion), kind=kCustom, calls=%fused_computation.2.clone | custom fusion | bytes 745472 | tf_op jit(solution)/shard_map/jit(_take)/gather | solution.py:60
  234.4 10.3 select_bitcast_fusion.2
  244.7 9.4 copy.243
  254.6 3.1 collective-permute-start.8
  259.1 3.0 collective-permute-done.9
  264.0 5.7 collective-permute-start.10
  270.7 7.0 gather_fusion.2
  281.1 86.7 %all-reduce.3 = (f32[]{:T(128)}, f32[]{:T(128)}) all-reduce(f32[]{:T(128)} %get-tuple-element.15, f32[]{:T(128)} %get-tuple-element.14), channel_id=1, replica_groups=mesh['region'=4,'member'=64] {'region','member'}, use_global_device_ids=true, to_apply=%region_8.10 | all-reduce | flops 2 | bytes 16 | tf_op jit(solution)/shard_map/psum | solution.py:85
  372.5 3.0 collective-permute-done.13
  375.5 4.0 collective-permute-start.15
  382.9 7.0 gather_fusion.3
  393.0 77.8 %all-reduce.2 = (f32[]{:T(128)}, f32[]{:T(128)}) all-reduce(f32[]{:T(128)} %get-tuple-element.13, f32[]{:T(128)} %get-tuple-element.12), channel_id=1, replica_groups=mesh['region'=4,'member'=64] {'region','member'}, use_global_device_ids=true, to_apply=%region_16.19 | all-reduce | flops 2 | bytes 16 | tf_op jit(solution)/shard_map/psum | solution.py:91
  475.3 74.8 %psum.88 = f32[]{:T(128)} all-reduce(f32[]{:T(128)} %multiply_reduce_fusion.24), channel_id=1, replica_groups=mesh['region'=4,'member'=64] {'region','member'}, use_global_device_ids=true, to_apply=%region_20.23 | all-reduce | flops 1 | bytes 8 | tf_op jit(solution)/shard_map/psum | solution.py:98
  551.5 3.0 collective-permute-start.16
  555.9 3.0 collective-permute-done.17
  558.8 4.0 collective-permute-start.19
  566.2 7.0 gather_fusion.4
  576.4 75.0 %psum.89 = f32[]{:T(128)} all-reduce(f32[]{:T(128)} %get-tuple-element.29), channel_id=1, replica_groups=mesh['region'=4,'member'=64] {'region','member'}, use_global_device_ids=true, to_apply=%region_24.27 | all-reduce | flops 1 | bytes 8 | tf_op jit(solution)/shard_map/psum | solution.py:88
  656.8 3.0 collective-permute-done.21
  659.7 4.0 collective-permute-start.23
  667.1 7.0 gather_fusion.5
  677.3 77.3 %all-reduce.1 = (f32[]{:T(128)}, f32[]{:T(128)}) all-reduce(f32[]{:T(128)} %get-tuple-element.11, f32[]{:T(128)} %get-tuple-element.10), channel_id=1, replica_groups=mesh['region'=4,'member'=64] {'region','member'}, use_global_device_ids=true, to_apply=%region_28.31 | all-reduce | flops 2 | bytes 16 | tf_op jit(solution)/shard_map/psum | solution.py:91
  759.1 74.8 %psum.92 = f32[]{:T(128)} all-reduce(f32[]{:T(128)} %get-tuple-element.26), channel_id=1, replica_groups=mesh['region'=4,'member'=64] {'region','member'}, use_global_device_ids=true, to_apply=%region_32.35 | all-reduce | flops 1 | bytes 8 | tf_op jit(solution)/shard_map/psum | solution.py:98
  839.3 3.0 collective-permute-done.25
  842.3 4.0 collective-permute-start.27
  849.6 7.0 gather_fusion.6
  859.7 75.0 %psum.93 = f32[]{:T(128)} all-reduce(f32[]{:T(128)} %get-tuple-element.24), channel_id=1, replica_groups=mesh['region'=4,'member'=64] {'region','member'}, use_global_device_ids=true, to_apply=%region_36.39 | all-reduce | flops 1 | bytes 8 | tf_op jit(solution)/shard_map/psum | solution.py:88
  940.1 3.0 collective-permute-done.29
  943.1 4.0 collective-permute-start.31
  950.5 7.0 gather_fusion.7
  960.7 77.3 %all-reduce = (f32[]{:T(128)}, f32[]{:T(128)}) all-reduce(f32[]{:T(128)} %get-tuple-element.9, f32[]{:T(128)} %get-tuple-element.8), channel_id=1, replica_groups=mesh['region'=4,'member'=64] {'region','member'}, use_global_device_ids=true, to_apply=%region_40.43 | all-reduce | flops 2 | bytes 16 | tf_op jit(solution)/shard_map/psum | solution.py:91
  1046.6 4.0 collective-permute-start.35
  1054.2 88.1 %gather_fusion.8 = f32[26624,3]{1,0:T(8,128)} fusion(f32[3,1280]{0,1:T(8,128)S(1)} %copy.277, s32[26624]{0:T(1024)S(1)} %copy-done.3), kind=kCustom, calls=%fused_computation.3.clone | custom fusion | bytes 745472 | tf_op jit(solution)/shard_map/jit(_take)/gather | solution.py:60
  1142.3 10.3 select_bitcast_fusion.1
  1152.6 9.4 copy.278
  1166.5 3.0 collective-permute-done.37
  1172.5 4.6 collective-permute-start.38
  1178.7 88.1 %gather_fusion.9 = f32[26624,3]{1,0:T(8,128)} fusion(f32[3,1280]{0,1:T(8,128)S(1)} %copy.282, s32[26624]{0:T(1024)S(1)} %copy-done.3), kind=kCustom, calls=%fused_computation.4.clone | custom fusion | bytes 745472 | tf_op jit(solution)/shard_map/jit(_take)/gather | solution.py:60
  1266.8 10.3 select_bitcast_fusion
  1277.1 9.4 copy.283
  (294 shorter events, 96.4 us)
Async XLA Ops:
  1.6 132.4 %copy-start.4 = (f32[1,3,3,1024]{3,0,2,1:T(1,128)}, f32[1,3,3,1024]{3,0,2,1:T(1,128)S(1)}, u32[]{:S(2)}) copy-start(f32[1,3,3,1024]{3,0,2,1:T(1,128)S(1)} %slice.176) | copy-start | bytes 110596
  2.6 125.8 %copy-start.9 = (f32[3,3,1024]{2,1,0:T(4,128)}, f32[3,3,1024]{2,1,0:T(4,128)S(1)}, u32[]{:S(2)}) copy-start(f32[3,3,1024]{2,1,0:T(4,128)S(1)} %get-tuple-element.34) | copy-start | bytes 110596
  2.6 10.1 collective-permute-start
  6.6 6.2 collective-permute-start.1
  9.7 224.7 %copy-start.7 = (pred[26,1024]{1,0:T(8,128)(4,1)}, pred[26,1024]{1,0:T(8,128)(4,1)S(1)}, u32[]{:S(2)}) copy-start(pred[26,1024]{1,0:T(8,128)(4,1)S(1)} %compare_and_fusion) | copy-start | bytes 79876
  11.8 134.4 %copy-start.2 = (s32[26624]{0:T(1024)}, s32[26624]{0:T(1024)S(1)}, u32[]{:S(2)}) copy-start(s32[26624]{0:T(1024)S(1)} %broadcast_clamp_fusion) | copy-start | bytes 319492
  12.7 246.3 %copy-start.15 = (f32[1,3,3,128]{3,0,2,1:T(1,128)}, f32[1,3,3,128]{3,0,2,1:T(1,128)S(1)}, u32[]{:S(2)}) copy-start(f32[1,3,3,128]{3,0,2,1:T(1,128)S(1)} %slice.195) | copy-start | bytes 13828
  12.8 6.0 collective-permute-start.3
  15.7 4.2 collective-permute-start.2
  128.4 106.0 %copy-start.18 = (f32[1,1,3,1024]{3,2,1,0:T(4,128)}, f32[1,1,3,1024]{3,2,1,0:T(4,128)S(1)}, u32[]{:S(2)}) copy-start(f32[1,1,3,1024]{3,2,1,0:T(4,128)S(1)} %bitcast_add_fusion.1) | copy-start | bytes 36868
  128.4 5.7 collective-permute-start.4
  132.7 4.7 collective-permute-start.5
  134.0 100.4 %copy-start.13 = (f32[3,1024]{1,0:T(4,128)}, f32[3,1024]{1,0:T(4,128)S(1)}, u32[]{:S(2)}) copy-start(f32[3,1024]{1,0:T(4,128)S(1)} %multiply_add_fusion.1) | copy-start | bytes 36868
  137.4 7.4 collective-permute-start.7
  139.7 6.1 collective-permute-start.6
  254.6 4.5 collective-permute-start.8
  257.7 4.3 collective-permute-start.9
  262.0 7.6 collective-permute-start.11
  264.0 6.4 collective-permute-start.10
  369.2 3.3 collective-permute-start.12
  371.1 4.3 collective-permute-start.13
  375.5 6.0 collective-permute-start.15
  379.5 3.1 collective-permute-start.14
  551.5 4.3 collective-permute-start.16
  554.5 4.3 collective-permute-start.17
  558.8 5.9 collective-permute-start.19
  562.8 3.1 collective-permute-start.18
  652.7 4.1 collective-permute-start.20
  655.4 4.3 collective-permute-start.21
  659.7 6.1 collective-permute-start.23
  663.7 3.1 collective-permute-start.22
  835.4 3.9 collective-permute-start.24
  837.9 4.3 collective-permute-start.25
  842.3 5.9 collective-permute-start.27
  846.3 3.1 collective-permute-start.26
  936.0 4.1 collective-permute-start.28
  938.8 4.3 collective-permute-start.29
  943.1 5.9 collective-permute-start.31
  947.1 3.1 collective-permute-start.30
  1039.6 4.0 collective-permute-start.32
  1042.1 4.5 collective-permute-start.33
  1046.6 6.0 collective-permute-start.35
  1050.6 3.1 collective-permute-start.34
  1162.3 4.2 collective-permute-start.36
  1165.1 4.5 collective-permute-start.37
  1166.4 100.3 %copy-start.20 = (f32[3,1024]{1,0:T(4,128)}, f32[3,1024]{1,0:T(4,128)S(1)}, u32[]{:S(2)}) copy-start(f32[3,1024]{1,0:T(4,128)S(1)} %multiply_add_fusion) | copy-start | bytes 36868
  1169.6 7.6 collective-permute-start.39
  1172.5 5.7 collective-permute-start.38
  (13 other events, 591.2 us)
where the time goes:
time: 1290 us
  blocking collectives  619 us (48%)
  local copies, waits for them, and re-layouts  442 us (34%)
  starting transfers between devices  107 us (8%)
  other arithmetic  64.5 us (5%)
  waiting for transfers between devices  37 us (3%)
  between operations  18.1 us (1%)
    gather x10, local copies, waits for them, and re-layouts, apply_index(): values = jnp.transpose(jnp.take(extended, index, axis=1), (1, 0, 2))  394 us
    psum x3, blocking collectives, body(): lax.psum((jnp.sum(second * middle), jnp.sum(second * second)), ('region',...  232 us
    psum x2, blocking collectives, body(): alpha = rho / lax.psum(jnp.sum(coarse_rhs * image), ('region', 'member'))  150 us
    psum x2, blocking collectives, body(): rho_new = lax.psum(jnp.sum(coarse_rhs * resid), ('region', 'member'))  150 us
    psum x1, blocking collectives, body(): rho = lax.psum(jnp.sum(resid * resid), ('region', 'member'))  86.7 us
    ppermute x20, starting transfers between devices, extended_2(): before = lax.ppermute(last, axis, up)  59.6 us
    transpose x10, other arithmetic, apply_index(): values = jnp.transpose(jnp.take(extended, index, axis=1), (1, 0, 2))  52.1 us
    ppermute x20, starting transfers between devices, extended_2(): after = lax.ppermute(leading, axis, down)  46.9 us
  transfers between devices with their start and end apart: 40, of which 19 were waited for; matrix products, arithmetic and copies ran while one was open for 0% of the time, Pallas kernels for 0%

commit v1 on v0

v1 whole, which is shorter than its diff:
```python
import functools

import jax
import jax.numpy as jnp
from jax import lax
from jax.experimental import pallas as pl
from jax.experimental.pallas import tpu as pltpu
from jax.sharding import PartitionSpec as P

STEPS = 3
BASIS = 2 * STEPS + 1
RELAX = 0.6
SLOTS = 27
PAD = 32
UNROLL = 2
MESH = pl.DeviceIdType.MESH
OFFSETS = ((-1, -1), (-1, 1), (1, -1), (1, 1), (0, 2), (2, 0), (0, -1), (0, 1), (-1, 0), (1, 0))
F32 = jnp.float32


def lanes_of(shape):
    return lax.broadcasted_iota(jnp.int32, shape, len(shape) - 1)


def rows_of(shape):
    return lax.broadcasted_iota(jnp.int32, shape, len(shape) - 2)


def take(table, index):
    return jnp.take_along_axis(table, index, axis=1, mode="promise_in_bounds")


def spread(row):
    return jnp.broadcast_to(row, (8, 128))


def combine(accs):
    rows = rows_of((8, 128))
    sums = [jnp.sum(acc, axis=0, keepdims=True) for acc in accs]
    tile = jnp.where(rows & 3 == 2, sums[2], 0.0)
    tile = jnp.where(rows & 3 == 1, sums[1], tile)
    return jnp.where(rows & 3 == 0, sums[0], tile)


def combine_pair(accs):
    return jnp.where(rows_of((8, 128)) < 4, combine(accs[:3]), combine(accs[3:]))


def coefficients(gram, shift):
    def image(x):
        y = [None] * (len(x) + 1)
        for i, value in enumerate(x):
            y[i] = value * shift if y[i] is None else y[i] + value * shift
            y[i + 1] = value
        return y

    def dot(x, y):
        terms = []
        for i, left in enumerate(x):
            inner = None
            for j, right in enumerate(y):
                term = gram[min(i, j), max(i, j)] * right
                inner = term if inner is None else inner + term
            terms.append(left * inner)
        return functools.reduce(lambda a, b: a + b, terms)

    def axpy(x, a, y):
        out = []
        for i in range(max(len(x), len(y))):
            if i >= len(y):
                out.append(x[i])
            elif i >= len(x):
                out.append(a * y[i])
            else:
                out.append(x[i] + a * y[i])
        return out

    def shadow(x):
        total = gram[0, 0] * x[0]
        for j in range(1, len(x)):
            total = total + gram[0, j] * x[j]
        return total

    one = jnp.ones_like(shift)
    resid, direction = [one], [one]
    error = []
    rho = gram[0, 0]
    for step in range(STEPS):
        move = image(direction)
        alpha = rho / shadow(move)
        middle = axpy(resid, -alpha, move)
        second = image(middle)
        omega = dot(second, middle) / dot(second, second)
        error = axpy(axpy(error, alpha, direction), omega, middle)
        if step + 1 < STEPS:
            resid = axpy(middle, -omega, second)
            rho_new = shadow(resid)
            beta = rho_new / rho * (alpha / omega)
            direction = axpy(resid, beta, axpy(direction, -omega, move))
            rho = rho_new
    return error


def kernel(
    regions, depth_y, depth_z, fine_dev, coarse_dev,
    rhs_hbm, fb_hbm, fl_hbm, cb_hbm, cl_hbm,
    both_out,
    rhs_raw, fb, fb_tail, fbh, fl, fl_tail, cb_raw, cb, cl, cidx, inv, rhs, fa, fc, fd, fa_image, steps, step_images, fl_halo, lift, pairs, images, tab, kv,
    hsend, hrecv, ksend, krecv, bsend, brecv, isend, irecv, fcb, e1, e2, g1, g2, row_send,
    load_sem, halo_send_sem, halo_recv_sem, k_send_sem, k_recv_sem, b_send_sem, b_recv_sem,
    red_send_sem, red_recv_sem,
):
    members = depth_y * depth_z * 2
    tiles = fine_dev // 128
    region = lax.axis_index("region")
    member = lax.axis_index("member")
    z, y, core = lax.div(member, 2 * depth_y), lax.rem(lax.div(member, 2), depth_y), lax.rem(member, 2)
    n1, n2 = regions * depth_y, depth_z * 2
    me1, me2 = region * depth_y + y, z * 2 + core
    region_at = [region] + [lax.rem(region + s, regions) for s in range(1, regions)]
    y_at = [member] + [member + 2 * (lax.rem(y + s, depth_y) - y) for s in range(1, depth_y)]
    z_at = [member] + [member + 2 * depth_y * (lax.rem(z + s, depth_z) - z) for s in range(1, depth_z)]
    peers1 = [(r, m) for r in region_at for m in y_at][1:]
    peers2 = [(region, m + flip) for m in z_at for flip in (0, 1 - 2 * core)][1:]

    def at(dr, dm):
        r = region if dr == 0 else lax.rem(region + (regions + dr), regions)
        m = member if dm == 0 else lax.rem(member + (members + dm), members)
        return r, m

    after, before, above, below = at(0, 1), at(0, -1), at(1, 0), at(-1, 0)

    loads = [
        pltpu.make_async_copy(rhs_hbm, rhs_raw, load_sem.at[4]),
        pltpu.make_async_copy(fb_hbm, fb, load_sem.at[0]),
        pltpu.make_async_copy(cb_hbm, cb_raw, load_sem.at[1]),
        pltpu.make_async_copy(cl_hbm, cl, load_sem.at[2]),
        pltpu.make_async_copy(fl_hbm, fl, load_sem.at[3]),
    ]
    loads[0].start()
    for i in range(3):
        for j in range(3):
            pltpu.make_async_copy(fb_hbm.at[i, j], fb.at[i, j], load_sem.at[0]).start()
    for load in loads[2:]:
        load.start()

    barrier = pltpu.get_barrier_semaphore()
    for dr, dm in OFFSETS:
        device = at(-dr, -dm)
        pl.semaphore_signal(barrier, inc=1, device_id=device, device_id_type=MESH)

    for device in peers1 + peers2:
        pl.semaphore_signal(barrier, inc=1, device_id=device, device_id_type=MESH)

    lane = lanes_of((8, 128))
    rows = rows_of((8, 128))

    def halo_copies(ex, which):
        pairs = (
            (1, 0, after),
            (0, 1, before),
            (0, 2, above),
            (0, 3, below),
        )
        return [
            pltpu.make_async_remote_copy(
                src_ref=hsend.at[2 * ex + src],
                dst_ref=hrecv.at[4 * ex + dst],
                send_sem=halo_send_sem,
                recv_sem=halo_recv_sem.at[ex],
                device_id=device,
                device_id_type=MESH,
            )
            for src, dst, device in pairs
            if src in which
        ]

    def halo_send(ex, first, last):
        hsend[2 * ex] = first
        hsend[2 * ex + 1] = last
        for copy in halo_copies(ex, (0, 1)):
            copy.start()

    def halo_wait(ex):
        block = hrecv.at[pl.ds(4 * ex, 4)]
        pltpu.make_async_copy(block, block, halo_recv_sem.at[ex]).wait()
        return [hrecv[4 * ex + k] for k in range(4)]

    def reduce_start(which, buffer, peers, me, value):
        row_send[which] = value
        buffer[me] = value
        for device in peers:
            pltpu.make_async_remote_copy(
                src_ref=row_send.at[which],
                dst_ref=buffer.at[me],
                send_sem=red_send_sem,
                recv_sem=red_recv_sem.at[which],
                device_id=device,
                device_id_type=MESH,
            ).start()

    def reduce_wait(which, buffer, count, op):
        block = buffer.at[pl.ds(0, count - 1)]
        pltpu.make_async_copy(block, block, red_recv_sem.at[which]).wait()
        return functools.reduce(op, [buffer[k] for k in range(count)])

    def smooth(value, columns=slice(None)):
        total = inv[0, :, columns] * value[0:1, :]
        for j in range(1, 3):
            total = total + inv[j, :, columns] * value[j : j + 1, :]
        return total

    def links(g, columns):
        return fl[8 * g : 8 * g + 8, columns] if g < 3 else fl_tail[:, columns]

    def blocks_at(i, j, g, columns):
        return fb[i, j, 8 * g : 8 * g + 8, columns] if g < 3 else fb_tail[i, j, :, columns]

    def fine_local(source, target, count=1):
        for n in range(count):
            for j in range(3):
                for r in range(tiles):
                    row = 4 * n + j
                    tab[3 * n + j, r] = spread(source[row : row + 1, 128 * r : 128 * r + 128])

        def tile(t, carry):
            columns = pl.ds(pl.multiple_of(t * 128, 128), 128)
            accs = [None] * (3 * count)
            for g in range(4):
                index = links(g, columns)
                where = index & 127
                bits = [(index & (128 << k)) != 0 for k in range(3)]
                for j in range(3):
                    values = []
                    for n in range(count):
                        found = [take(tab[3 * n + j, r], where) for r in range(tiles)]
                        for bit in bits:
                            found = [
                                jnp.where(bit, found[2 * q + 1], found[2 * q])
                                for q in range(len(found) // 2)
                            ]
                        values.append(found[0])
                    for i in range(3):
                        block = blocks_at(i, j, g, columns)
                        for n in range(count):
                            term = block * values[n]
                            k = 3 * n + i
                            accs[k] = term if accs[k] is None else accs[k] + term
            for k in range(3 * count):
                pairs[k, t] = accs[k]
            return carry

        lax.fori_loop(0, tiles, tile, 0, unroll=UNROLL if count == 1 else 1)
        for t in range(tiles):
            sums = [pairs[k, t] for k in range(3 * count)]
            target[:, 128 * t : 128 * t + 128] = combine(sums) if count == 1 else combine_pair(sums)

    def fine_remote(halves):
        accs = [None] * 3
        for g in range(4):
            part = slice(8 * g, 8 * g + 8)
            index = links(g, slice(0, 128))
            where = index & 127
            bit = (index & 128) != 0
            for j in range(3):
                low, high = (take(spread(half[j : j + 1, :]), where) for half in halves)
                value = jnp.where(bit, high, low)
                for i in range(3):
                    term = fbh[i, j, part, :] * value
                    accs[i] = term if accs[i] is None else accs[i] + term
        return combine(accs)

    def fine_send(ex, field):
        within = lane & 63
        halo_send(
            ex,
            take(field[:, 0:128], within),
            take(field[:, fine_dev - 128 : fine_dev], within + 64),
        )

    def fine_wait(ex):
        left, right, lower, upper = halo_wait(ex)
        return jnp.where(lane < 64, left, right), jnp.where(lane < 64, lower, upper)

    rhs[...] = jnp.zeros((8, fine_dev), F32)
    loads[0].wait()
    rhs[0:3, :] = rhs_raw[...]
    rhs[4:7, :] = rhs_raw[...]
    loads[1].wait()

    def start_tile(t, carry):
        columns = pl.ds(pl.multiple_of(t * 128, 128), 128)
        (a, b, c), (d, e, f), (g_, h_, i_) = [
            [spread(fb[i, j, 26:27, columns]) for j in range(3)] for i in range(3)
        ]
        co_a = e * i_ - f * h_
        co_b = f * g_ - d * i_
        co_c = d * h_ - e * g_
        scale = RELAX / (a * co_a + b * co_b + c * co_c)
        adjugate = [
            [co_a, c * h_ - b * i_, b * f - c * e],
            [co_b, a * i_ - c * g_, c * d - a * f],
            [co_c, b * g_ - a * h_, a * e - b * d],
        ]
        total = None
        for j in range(3):
            column = jnp.where(rows & 3 == 2, adjugate[2][j], 0.0)
            column = jnp.where(rows & 3 == 1, adjugate[1][j], column)
            column = jnp.where(rows & 3 == 0, adjugate[0][j], column) * scale
            inv[j, :, columns] = column
            term = column * spread(rhs[j : j + 1, columns])
            total = term if total is None else total + term
        fa[:, columns] = total
        return carry

    lax.fori_loop(0, tiles, start_tile, 0, unroll=UNROLL)
    pl.semaphore_wait(barrier, len(OFFSETS) + (n1 - 1) + (n2 - 1))
    fine_send(0, fa)

    fl_tail[...] = jnp.where(rows_of((8, fine_dev)) == 2, lanes_of((8, fine_dev)), 0)
    fb_tail[...] = jnp.zeros((3, 3, 8, fine_dev), F32)
    fb_tail[:, :, 0:3, :] = fb[:, :, 24:27, :]
    loads[4].wait()
    fl_tail[0:2, :] = fl[24:26, :]
    for g in range(4):
        part = slice(8 * g, 8 * g + 8)
        outside = links(g, slice(0, 128)) >= fine_dev
        for i in range(3):
            for j in range(3):
                block = blocks_at(i, j, g, slice(0, 128))
                fbh[i, j, part, :] = jnp.where(outside, block, 0.0)
                inside = jnp.where(outside, 0.0, block)
                if g < 3:
                    fb[i, j, part, 0:128] = inside
                else:
                    fb_tail[i, j, :, 0:128] = inside

    kv[...] = jnp.zeros((3, 8, 128), F32)
    cidx[24:32, :] = jnp.where(rows == 2, lane, 0)
    cb[:, :, 24:32, :] = jnp.zeros((3, 3, 8, 128), F32)
    loads[2].wait()
    loads[3].wait()
    cb[:, :, 0:27, :] = cb_raw[...]
    cidx[0:26, :] = cl[...]
    diagonal = [cb[i, i, 26:27, :] for i in range(3)]
    largest = functools.reduce(jnp.maximum, diagonal)
    smallest = -functools.reduce(jnp.minimum, diagonal)
    largest, smallest = spread(largest), spread(smallest)
    swap = lane ^ 64
    largest = jnp.maximum(largest, take(largest, swap))
    smallest = jnp.maximum(smallest, take(smallest, swap))
    extremes = jnp.where(lane < 64, largest, smallest)[0:1]

    reduce_start(0, e1, peers1, me1, extremes)
    fine_local(fa, fc)

    quarter = lane >> 5

    def packed(pieces, start):
        rolled = [pltpu.roll(piece, (128 + 32 * g - start) % 128, 1) for g, piece in enumerate(pieces)]
        low = jnp.where(quarter == 0, rolled[0], rolled[1])
        return jnp.where(quarter < 2, low, jnp.where(quarter == 2, rolled[2], rolled[3]))

    parts = [slice(8 * g, 8 * g + 8) for g in range(4)]
    codes = [cidx[part, :] for part in parts]
    for end, start in ((0, 0), (1, coarse_dev - 32)):
        isend[end] = packed(codes, start)
        for i in range(3):
            for j in range(3):
                bsend[end, 3 * i + j] = packed([cb[i, j, part, :] for part in parts], start)
    face_code = isend[0]
    for i in range(3):
        for j in range(3):
            fcb[i, j] = jnp.where(face_code >= coarse_dev, bsend[0, 3 * i + j], 0.0)
            for g in range(4):
                cb[i, j, parts[g], :] = jnp.where(codes[g] >= coarse_dev, 0.0, cb[i, j, parts[g], :])
    for g in range(4):
        cidx[parts[g], :] = codes[g] & 127
    side_copies = []
    for src, dst, device in ((1, 0, after), (0, 1, before), (0, 2, above), (0, 3, below)):
        for kind, (source, sink) in enumerate(((bsend, brecv), (isend, irecv))):
            side_copies.append(
                pltpu.make_async_remote_copy(
                    src_ref=source.at[src],
                    dst_ref=sink.at[dst],
                    send_sem=b_send_sem.at[kind],
                    recv_sem=b_recv_sem.at[kind],
                    device_id=device,
                    device_id_type=MESH,
                )
            )
    for copy in side_copies:
        copy.start()
    head, rest = slice(0, 128), slice(128, fine_dev)
    fa[:, rest] += smooth(rhs[:, rest] - fc[:, rest], rest)
    halves = fine_wait(0)
    fa[:, head] += smooth(rhs[:, head] - fc[:, head] - fine_remote(halves), head)
    fine_send(1, fa)
    extremes = reduce_wait(0, e1, n1, jnp.maximum)
    reduce_start(1, e2, peers2, me2, extremes)
    fine_local(fa, fc)

    def eighths(part):
        for k in (1, 2, 4):
            part = part + pltpu.roll(part, 128 - k, 1)
        return take(part, (lane & 15) * 8)

    def restrict(ref):
        out = eighths(ref[:, 0:128])
        for t in range(1, tiles):
            picked = eighths(ref[:, 128 * t : 128 * t + 128])
            out = jnp.where(lane >> 4 == t, picked, out)
        return out

    fc[...] = rhs[...] - fc[...]
    coarse = restrict(fc)
    remote = fine_remote(fine_wait(1))
    fc[:, head] -= remote
    coarse = coarse - jnp.where(lane < 16, eighths(remote), 0.0)

    def coarse_send(ex, field):
        edge = take(field, jnp.where(lane < 32, lane + (coarse_dev - 32), lane & 31))
        tile = jnp.where(rows < 4, field, edge)
        ksend[ex] = tile
        for k, (dr, dm) in enumerate(OFFSETS):
            pltpu.make_async_remote_copy(
                src_ref=ksend.at[ex],
                dst_ref=krecv.at[ex, k],
                send_sem=k_send_sem,
                recv_sem=k_recv_sem.at[ex],
                device_id=at(-dr, -dm),
                device_id_type=MESH,
            ).start()
        return tile

    def coarse_wait(ex):
        block = krecv.at[ex]
        pltpu.make_async_copy(block, block, k_recv_sem.at[ex]).wait()
        return {offset: krecv[ex, k] for k, offset in enumerate(OFFSETS)}

    def beside(left, right, lower, upper):
        low = jnp.where(quarter == 0, left, right)
        return jnp.where(quarter < 2, low, jnp.where(quarter == 2, lower, upper))

    def folded(accs):
        tile = combine(accs)
        tile = tile + pltpu.roll(tile, 64, 1)
        return tile + pltpu.roll(tile, 32, 1)

    def coarse_local(field):
        accs = [None] * 3
        tables = [spread(field[j : j + 1, :]) for j in range(3)]
        for g in range(4):
            index = cidx[parts[g], :]
            for j in range(3):
                value = take(tables[j], index)
                for i in range(3):
                    term = cb[i, j, parts[g], :] * value
                    accs[i] = term if accs[i] is None else accs[i] + term
        return combine(accs)

    def coarse_remote(halo):
        accs = [None] * 3
        index = isend[0] & 127
        for j in range(3):
            value = take(spread(halo[4 + j : 5 + j, :]), index)
            for i in range(3):
                term = fcb[i, j] * value
                accs[i] = term if accs[i] is None else accs[i] + term
        return jnp.where(lane < 32, folded(accs), 0.0)

    def coarse_ghost(tiles_of, mine):
        around = (
            ((0, -1), None),
            ((0, 1), (mine, tiles_of[0, 2], tiles_of[-1, 1], tiles_of[1, 1])),
            ((-1, 0), (tiles_of[-1, -1], tiles_of[-1, 1], tiles_of[2, 0], mine)),
            ((1, 0), (tiles_of[1, -1], tiles_of[1, 1], mine, tiles_of[2, 0])),
        )
        out = None
        for q, (offset, edges) in enumerate(around):
            code = irecv[q]
            index = code & 127
            full = tiles_of[offset]
            outer = None if edges is None else beside(*edges)
            accs = [None] * 3
            for j in range(3):
                value = take(spread(full[j : j + 1, :]), index)
                if outer is not None:
                    far = take(spread(outer[4 + j : 5 + j, :]), index)
                    value = jnp.where(code >= coarse_dev, far, value)
                for i in range(3):
                    term = brecv[q, 3 * i + j] * value
                    accs[i] = term if accs[i] is None else accs[i] + term
            tile = folded(accs)
            out = tile if out is None else jnp.where(quarter == q, tile, out)
        return out

    def lift_pair(ex, fields, halos):
        for n in range(2):
            for j in range(3):
                lift[n, j] = spread(fields[n][j : j + 1, :])

        def tile(t, carry):
            columns = pl.ds(pl.multiple_of(t * 128, 128), 128)
            accs = [None] * 6
            for g in range(4):
                where = (links(g, columns) >> 3) & 127
                for j in range(3):
                    values = [take(lift[n, j], where) for n in range(2)]
                    for i in range(3):
                        block = blocks_at(i, j, g, columns)
                        for n in range(2):
                            term = block * values[n]
                            k = 3 * n + i
                            accs[k] = term if accs[k] is None else accs[k] + term
            for k in range(6):
                pairs[k, t] = accs[k]
            return carry

        lax.fori_loop(0, tiles, tile, 0, unroll=UNROLL)
        accs = [pairs[k, 0] for k in range(6)]
        for g in range(4):
            where = fl_halo[parts[g], :]
            for j in range(3):
                values = [take(spread(halos[n][4 + j : 5 + j, :]), where) for n in range(2)]
                for i in range(3):
                    block = fbh[i, j, parts[g], :]
                    for n in range(2):
                        accs[3 * n + i] = accs[3 * n + i] + block * values[n]
        images[ex, :, 0:128] = combine_pair(accs)
        for t in range(1, tiles):
            images[ex, :, 128 * t : 128 * t + 128] = combine_pair([pairs[k, t] for k in range(6)])

        def faces(columns):
            total = None
            for j in range(3):
                value = jnp.where(
                    rows < 4, spread(images[ex, j : j + 1, columns]), spread(images[ex, j + 4 : j + 5, columns])
                )
                term = inv[j, :, columns] * value
                total = term if total is None else total + term
            return total

        for t in range(tiles):
            columns = slice(128 * t, 128 * t + 128)
            steps[:, columns] = faces(columns)
        fine_send(3 + ex, steps)

    mine = coarse_send(0, coarse)
    for g in range(4):
        node = links(g, slice(0, 128)) & 255
        fl_halo[parts[g], :] = ((node >> 6) << 5) + ((node & 63) >> 3) + jnp.where(node < 64, 24, 0)
    update = smooth(fc[...])
    fd[...] = update
    fine_send(2, fd)
    fine_local(fd, fa_image)
    extremes = spread(reduce_wait(1, e2, n2, jnp.maximum))
    lowest = jnp.min(extremes)
    largest = jnp.max(jnp.where(lane < 64, extremes, lowest), axis=1, keepdims=True)
    smallest = -jnp.max(jnp.where(lane < 64, lowest, extremes), axis=1, keepdims=True)
    largest, smallest = jnp.broadcast_to(largest, (8, 128)), jnp.broadcast_to(smallest, (8, 128))
    centre = 0.5 * largest + 0.5 * smallest
    width = 0.5 * largest - 0.5 * smallest + 0.125 * largest
    shrink = 1.0 / width
    for kind, sink in enumerate((brecv, irecv)):
        pltpu.make_async_copy(sink, sink, b_recv_sem.at[kind]).wait()

    def keep(ref, k, field):
        for j in range(3):
            ref[j, k : k + 1, :] = field[j : j + 1, :]

    for ex in range(STEPS):
        local = coarse_local(coarse) - centre * coarse
        keep(kv, 2 * ex, coarse)
        base = coarse
        tiles_of = coarse_wait(ex)
        halo = beside(tiles_of[0, -1], tiles_of[0, 1], tiles_of[-1, 0], tiles_of[1, 0])
        coarse = (local + coarse_remote(halo)) * shrink
        ghost = (coarse_ghost(tiles_of, mine) - centre * halo) * shrink
        keep(kv, 2 * ex + 1, coarse)
        pair = (base, coarse), (halo, ghost)
        coarse = (coarse_local(coarse) - centre * coarse + coarse_remote(ghost)) * shrink
        if ex + 1 < STEPS:
            mine = coarse_send(ex + 1, coarse)
            lift_pair(ex, *pair)
            fine_local(steps, step_images.at[ex], 2)
    for j in range(3):
        kv[j, BASIS - 1 : BASIS, :] = coarse[j : j + 1, :]

    basis = jnp.concatenate([kv[0], kv[1], kv[2]], axis=1)
    gram = lax.dot_general(
        basis, basis, (((1,), (1,)), ((), ())),
        precision=lax.Precision.HIGHEST, preferred_element_type=F32,
    )
    gram = jnp.concatenate([gram, jnp.zeros((8, 120), F32)], axis=1)
    gram = jnp.where(rows == lane >> 3, take(gram, lane & 7), 0.0)
    gram = jnp.sum(gram, axis=0, keepdims=True)
    reduce_start(2, g1, peers1, me1, gram)
    lift_pair(STEPS - 1, *pair)
    gram = reduce_wait(2, g1, n1, jnp.add)
    reduce_start(3, g2, peers2, me2, gram)
    fine_local(steps, step_images.at[STEPS - 1], 2)
    gram = spread(reduce_wait(3, g2, n2, jnp.add))
    entries = {
        (i, j): take(gram, jnp.full((8, 128), 8 * i + j, jnp.int32))
        for i in range(BASIS)
        for j in range(i, BASIS)
    }
    weights = [weight * shrink for weight in coefficients(entries, centre * shrink)]

    def mix(ref):
        out = []
        for j in range(3):
            total = None
            for k, weight in enumerate(weights):
                term = weight[0:1] * ref[j, k : k + 1, :]
                total = term if total is None else total + term
            out.append(total)
        tile = jnp.where(rows == 1, out[1], jnp.where(rows == 2, out[2], 0.0))
        return jnp.where(rows == 0, out[0], tile)

    doubled = [jnp.where(rows < 4, weights[2 * ex], weights[2 * ex + 1]) for ex in range(STEPS)]

    def mix_pairs(tiles_of):
        total = functools.reduce(jnp.add, [w * tile for w, tile in zip(doubled, tiles_of)])
        return total + pltpu.roll(total, 4, 0)

    for t in range(tiles):
        columns = slice(128 * t, 128 * t + 128)
        fc[:, columns] = fc[:, columns] - mix_pairs([images[ex, :, columns] for ex in range(STEPS)])
    error = mix(kv)
    update = smooth(fc[...])
    low, high = fine_wait(2)
    others = [fine_wait(3 + ex) for ex in range(STEPS)]
    halves = [
        low - mix_pairs([other[0] for other in others]),
        high - mix_pairs([other[1] for other in others]),
    ]
    remote = fine_remote(halves)
    for t in range(tiles):
        columns = slice(128 * t, 128 * t + 128)
        both_out[0, :, columns] = (fa[:, columns] + update[:, columns] + take(error, 16 * t + (lane >> 3)))[0:3]
        final = fc[:, columns] - fa_image[:, columns]
        final = final + mix_pairs([step_images[ex, :, columns] for ex in range(STEPS)])
        both_out[1, :, columns] = (final - remote if t == 0 else final)[0:3]

    pltpu.make_async_copy(hrecv, hrecv, halo_send_sem).wait()
    pltpu.make_async_copy(krecv, krecv, k_send_sem).wait()
    for kind, sink in enumerate((brecv, irecv)):
        pltpu.make_async_copy(sink, sink, b_send_sem.at[kind]).wait()
    for buffer, count in ((e1, n1), (e2, n2), (g1, n1), (g2, n2)):
        block = buffer.at[pl.ds(0, count - 1)]
        pltpu.make_async_copy(block, block, red_send_sem).wait()


def body(regions, depth_y, depth_z, right_side, fine_blocks, fine_links, coarse_blocks, coarse_links):
    fine_dev, coarse_dev = right_side.shape[1], coarse_blocks.shape[3]
    n1, n2 = regions * depth_y, depth_z * 2
    exchanges = 3 + STEPS
    reach = len(OFFSETS)
    vmem = pl.BlockSpec(memory_space=pltpu.VMEM)
    hbm = pl.BlockSpec(memory_space=pltpu.HBM)
    out = pltpu.VMEM((2, 3, fine_dev), F32)
    both = pl.pallas_call(
        functools.partial(kernel, regions, depth_y, depth_z, fine_dev, coarse_dev),
        out_shape=out,
        in_specs=[hbm] * 5,
        out_specs=vmem,
        scratch_shapes=[
            pltpu.VMEM((3, fine_dev), F32),
            pltpu.VMEM((3, 3, SLOTS, fine_dev), F32),
            pltpu.VMEM((3, 3, 8, fine_dev), F32),
            pltpu.VMEM((3, 3, PAD, 128), F32),
            pltpu.VMEM((SLOTS - 1, fine_dev), jnp.int32),
            pltpu.VMEM((8, fine_dev), jnp.int32),
            pltpu.VMEM((3, 3, SLOTS, 128), F32),
            pltpu.VMEM((3, 3, PAD, 128), F32),
            pltpu.VMEM((SLOTS - 1, 128), jnp.int32),
            pltpu.VMEM((PAD, 128), jnp.int32),
            pltpu.VMEM((3, 8, fine_dev), F32),
            pltpu.VMEM((8, fine_dev), F32),
            pltpu.VMEM((8, fine_dev), F32),
            pltpu.VMEM((8, fine_dev), F32),
            pltpu.VMEM((8, fine_dev), F32),
            pltpu.VMEM((8, fine_dev), F32),
            pltpu.VMEM((8, fine_dev), F32),
            pltpu.VMEM((STEPS, 8, fine_dev), F32),
            pltpu.VMEM((PAD, 128), jnp.int32),
            pltpu.VMEM((2, 3, 8, 128), F32),
            pltpu.VMEM((6, fine_dev // 128, 8, 128), F32),
            pltpu.VMEM((STEPS, 8, fine_dev), F32),
            pltpu.VMEM((6, fine_dev // 128, 8, 128), F32),
            pltpu.VMEM((3, 8, 128), F32),
            pltpu.VMEM((2 * exchanges, 8, 128), F32),
            pltpu.VMEM((4 * exchanges, 8, 128), F32),
            pltpu.VMEM((STEPS, 8, 128), F32),
            pltpu.VMEM((STEPS, reach, 8, 128), F32),
            pltpu.VMEM((2, 9, 8, 128), F32),
            pltpu.VMEM((4, 9, 8, 128), F32),
            pltpu.VMEM((2, 8, 128), jnp.int32),
            pltpu.VMEM((4, 8, 128), jnp.int32),
            pltpu.VMEM((3, 3, 8, 128), F32),
            pltpu.VMEM((n1, 1, 128), F32),
            pltpu.VMEM((n2, 1, 128), F32),
            pltpu.VMEM((n1, 1, 128), F32),
            pltpu.VMEM((n2, 1, 128), F32),
            pltpu.VMEM((4, 1, 128), F32),
            pltpu.SemaphoreType.DMA((5,)),
            pltpu.SemaphoreType.DMA,
            pltpu.SemaphoreType.DMA((exchanges,)),
            pltpu.SemaphoreType.DMA,
            pltpu.SemaphoreType.DMA((STEPS,)),
            pltpu.SemaphoreType.DMA((2,)),
            pltpu.SemaphoreType.DMA((2,)),
            pltpu.SemaphoreType.DMA,
            pltpu.SemaphoreType.DMA((4,)),
        ],
        compiler_params=pltpu.CompilerParams(
            collective_id=0, has_side_effects=True, vmem_limit_bytes=60 * 1024 * 1024
        ),
    )(
        right_side,
        jnp.transpose(fine_blocks, (1, 2, 0, 3)),
        fine_links,
        jnp.transpose(coarse_blocks, (1, 2, 0, 3)),
        coarse_links,
    )
    return both[0], both[1]


def solution(mesh):
    regions, members = mesh.shape["region"], mesh.shape["member"]
    depth_y = 4 if members % 8 == 0 else 2
    depth_z = members // (2 * depth_y)
    flat = ("region", "member")
    return jax.shard_map(
        functools.partial(body, regions, depth_y, depth_z),
        mesh=mesh,
        in_specs=(
            P(None, flat),
            P(None, None, None, flat),
            P(None, flat),
            P(None, None, None, flat),
            P(None, flat),
        ),
        out_specs=(P(None, flat), P(None, flat)),
        check_vma=False,
    )
```

time: 1290 us -> 45.4 us (0.04)
  blocking collectives: 619 us -> 0 us
  local copies, waits for them, and re-layouts: 442 us -> 0.62 us
  starting transfers between devices: 107 us -> 0 us
  other arithmetic: 64.5 us -> 0 us
  Pallas kernels: 0 us -> 44 us
  waiting for transfers between devices: 37 us -> 0 us
  between operations: 18.1 us -> 0.64 us
    psum x8 -> x0, blocking collectives: 619 us -> none  [the longest x3 232 us: body(): lax.psum((jnp.sum(second * middle), jnp.sum(second * second)), ('region',...]
    gather x10 -> x0, local copies, waits for them, and re-layouts: 394 us -> none  [apply_index(): values = jnp.transpose(jnp.take(extended, index, axis=1), (1, 0, 2))]
    ppermute x40 -> x0, starting transfers between devices: 107 us -> none  [the longest x20 59.6 us: extended_2(): before = lax.ppermute(last, axis, up)]
    transpose x10 -> x0, other arithmetic: 52.1 us -> none  [apply_index(): values = jnp.transpose(jnp.take(extended, index, axis=1), (1, 0, 2))]
    pallas_call x0 -> x1, Pallas kernels: none -> 44 us  [body(): pl.pallas_call(functools.partial(kernel, regions, depth_y, depth_z, fine_...]
    transpose x10 -> x0, local copies, waits for them, and re-layouts: 41.3 us -> none  [apply_index(): values = jnp.transpose(jnp.take(extended, index, axis=1), (1, 0, 2))]
    ppermute x40 -> x0, waiting for transfers between devices: 37 us -> none  [the longest x20 27 us: extended_2(): after = lax.ppermute(leading, axis, down)]
  transfers between devices with their start and end apart: 40 -> 0, of which waited for: 19 -> 0; matrix products, arithmetic and copies ran while one was open for 0% -> 0% of each run, Pallas kernels for 0% -> 0%
where the time goes in v1:
time: 45.4 us; the launch traced here: 45.2 us
  Pallas kernels  44 us (97%)
  between operations  0.64 us (1%)
  local copies, waits for them, and re-layouts  0.62 us (1%)
    pallas_call x1, Pallas kernels, body(): pl.pallas_call(functools.partial(kernel, regions, depth_y, depth_z, fine_...  44 us

profile of v1, /device:TPU:1, one launch (start us, length us, event | category | flops | bytes accessed | tf_op | source)
XLA Modules:
  0.0 45.2 jit_solution(1435206791304129553)
XLA Ops:
  0.6 44.0 %shard_map.68 = f32[2,3,1024]{2,1,0:T(4,128)S(1)} custom-call(f32[3,1024]{1,0:T(4,128)} %rhs_hbm.1, f32[3,3,27,1024]{3,2,1,0:T(8,128)} %bitcast.6, s32[26,1024]{1,0:T(8,128)} %fl_hbm.1, f32[3,3,27,128]{3,2,1,0:T(8,128)} %bitcast.7, s32[26,128]{1,0:T(8,128)} %cl_hbm.1), custom_call_target="tpu_custom_call" | custom-call | tf_op jit(solution)/shard_map/pallas_call | solution.py:664
  44.6 0.6 %slice_bitcast_fusion = (f32[3,1024]{1,0:T(4,128)}, f32[3,1024]{1,0:T(4,128)}) fusion(f32[2,3,1024]{2,1,0:T(4,128)S(1)} %shard_map.68), kind=kLoop, calls=%fused_computation | loop fusion | bytes 49152 | tf_op jit(solution)/shard_map/squeeze | solution.py:728

commit v2 on v1

--- a/solution.py
+++ b/solution.py
@@ -54,15 +54,18 @@
             y[i + 1] = value
         return y
 
+    def total(terms):
+        while len(terms) > 1:
+            terms = [terms[k] + terms[k + 1] if k + 1 < len(terms) else terms[k] for k in range(0, len(terms), 2)]
+        return terms[0]
+
+    def products(x, count):
+        return [
+            total([gram[min(i, j), max(i, j)] * value for j, value in enumerate(x)]) for i in range(count)
+        ]
+
     def dot(x, y):
-        terms = []
-        for i, left in enumerate(x):
-            inner = None
-            for j, right in enumerate(y):
-                term = gram[min(i, j), max(i, j)] * right
-                inner = term if inner is None else inner + term
-            terms.append(left * inner)
-        return functools.reduce(lambda a, b: a + b, terms)
+        return total([left * right for left, right in zip(x, y)])
 
     def axpy(x, a, y):
         out = []
@@ -76,10 +79,7 @@
         return out
 
     def shadow(x):
-        total = gram[0, 0] * x[0]
-        for j in range(1, len(x)):
-            total = total + gram[0, j] * x[j]
-        return total
+        return total([gram[0, j] * value for j, value in enumerate(x)])
 
     one = jnp.ones_like(shift)
     resid, direction = [one], [one]
@@ -90,7 +90,8 @@
         alpha = rho / shadow(move)
         middle = axpy(resid, -alpha, move)
         second = image(middle)
-        omega = dot(second, middle) / dot(second, second)
+        against = products(second, len(second))
+        omega = dot(middle, against) / dot(second, against)
         error = axpy(axpy(error, alpha, direction), omega, middle)
         if step + 1 < STEPS:
             resid = axpy(middle, -omega, second)
@@ -120,8 +121,14 @@
     region_at = [region] + [lax.rem(region + s, regions) for s in range(1, regions)]
     y_at = [member] + [member + 2 * (lax.rem(y + s, depth_y) - y) for s in range(1, depth_y)]
     z_at = [member] + [member + 2 * depth_y * (lax.rem(z + s, depth_z) - z) for s in range(1, depth_z)]
-    peers1 = [(r, m) for r in region_at for m in y_at][1:]
-    peers2 = [(region, m + flip) for m in z_at for flip in (0, 1 - 2 * core)][1:]
+    def far_first(outer, inner, pair):
+        around = lambda s, count: min(s, count - s)
+        steps = [(s, t) for s in range(len(outer)) for t in range(len(inner))][1:]
+        steps.sort(key=lambda st: -around(st[0], len(outer)) - around(st[1], len(inner)))
+        return [pair(outer[s], inner[t]) for s, t in steps]
+
+    peers1 = far_first(region_at, y_at, lambda r, m: (r, m))
+    peers2 = far_first(z_at, [0, 1 - 2 * core], lambda m, flip: (region, m + flip))
 
     def at(dr, dm):
         r = region if dr == 0 else lax.rem(region + (regions + dr), regions)
@@ -255,20 +262,26 @@
             sums = [pairs[k, t] for k in range(3 * count)]
             target[:, 128 * t : 128 * t + 128] = combine(sums) if count == 1 else combine_pair(sums)
 
-    def fine_remote(halves):
-        accs = [None] * 3
+    def fine_remote(halves, count=1):
+        accs = [None] * (3 * count)
         for g in range(4):
             part = slice(8 * g, 8 * g + 8)
             index = links(g, slice(0, 128))
             where = index & 127
             bit = (index & 128) != 0
             for j in range(3):
-                low, high = (take(spread(half[j : j + 1, :]), where) for half in halves)
-                value = jnp.where(bit, high, low)
+                values = []
+                for n in range(count):
+                    row = 4 * n + j
+                    low, high = (take(spread(half[row : row + 1, :]), where) for half in halves)
+                    values.append(jnp.where(bit, high, low))
                 for i in range(3):
-                    term = fbh[i, j, part, :] * value
-                    accs[i] = term if accs[i] is None else accs[i] + term
-        return combine(accs)
+                    block = fbh[i, j, part, :]
+                    for n in range(count):
+                        term = block * values[n]
+                        k = 3 * n + i
+                        accs[k] = term if accs[k] is None else accs[k] + term
+        return combine(accs) if count == 1 else combine_pair(accs)
 
     def fine_send(ex, field):
         within = lane & 63
@@ -313,9 +326,11 @@
         fa[:, columns] = total
         return carry
 
-    lax.fori_loop(0, tiles, start_tile, 0, unroll=UNROLL)
+    start_tile(0, 0)
+    start_tile(tiles - 1, 0)
     pl.semaphore_wait(barrier, len(OFFSETS) + (n1 - 1) + (n2 - 1))
     fine_send(0, fa)
+    lax.fori_loop(1, tiles - 1, start_tile, 0, unroll=UNROLL)
 
     fl_tail[...] = jnp.where(rows_of((8, fine_dev)) == 2, lanes_of((8, fine_dev)), 0)
     fb_tail[...] = jnp.zeros((3, 3, 8, fine_dev), F32)
@@ -584,22 +599,28 @@
             mine = coarse_send(ex + 1, coarse)
             lift_pair(ex, *pair)
             fine_local(steps, step_images.at[ex], 2)
+            if ex == 1:
+                fa_image[:, head] += fine_remote(fine_wait(2))
+                step_images[0, :, head] += fine_remote(fine_wait(3), 2)
     for j in range(3):
         kv[j, BASIS - 1 : BASIS, :] = coarse[j : j + 1, :]
 
-    basis = jnp.concatenate([kv[0], kv[1], kv[2]], axis=1)
-    gram = lax.dot_general(
-        basis, basis, (((1,), (1,)), ((), ())),
-        precision=lax.Precision.HIGHEST, preferred_element_type=F32,
-    )
-    gram = jnp.concatenate([gram, jnp.zeros((8, 120), F32)], axis=1)
-    gram = jnp.where(rows == lane >> 3, take(gram, lane & 7), 0.0)
+    gram = jnp.zeros((8, 128), F32)
+    for k in range(BASIS):
+        column = None
+        for j in range(3):
+            term = kv[j] * spread(kv[j, k : k + 1, :])
+            column = term if column is None else column + term
+        gram = jnp.where(lane & 7 == k, jnp.sum(column, axis=1, keepdims=True), gram)
+    gram = jnp.where(rows == lane >> 3, gram, 0.0)
     gram = jnp.sum(gram, axis=0, keepdims=True)
     reduce_start(2, g1, peers1, me1, gram)
     lift_pair(STEPS - 1, *pair)
     gram = reduce_wait(2, g1, n1, jnp.add)
     reduce_start(3, g2, peers2, me2, gram)
     fine_local(steps, step_images.at[STEPS - 1], 2)
+    for ex in range(1, STEPS):
+        step_images[ex, :, head] += fine_remote(fine_wait(3 + ex), 2)
     gram = spread(reduce_wait(3, g2, n2, jnp.add))
     entries = {
         (i, j): take(gram, jnp.full((8, 128), 8 * i + j, jnp.int32))
@@ -630,19 +651,12 @@
         fc[:, columns] = fc[:, columns] - mix_pairs([images[ex, :, columns] for ex in range(STEPS)])
     error = mix(kv)
     update = smooth(fc[...])
-    low, high = fine_wait(2)
-    others = [fine_wait(3 + ex) for ex in range(STEPS)]
-    halves = [
-        low - mix_pairs([other[0] for other in others]),
-        high - mix_pairs([other[1] for other in others]),
-    ]
-    remote = fine_remote(halves)
     for t in range(tiles):
         columns = slice(128 * t, 128 * t + 128)
         both_out[0, :, columns] = (fa[:, columns] + update[:, columns] + take(error, 16 * t + (lane >> 3)))[0:3]
         final = fc[:, columns] - fa_image[:, columns]
         final = final + mix_pairs([step_images[ex, :, columns] for ex in range(STEPS)])
-        both_out[1, :, columns] = (final - remote if t == 0 else final)[0:3]
+        both_out[1, :, columns] = final[0:3]
 
     pltpu.make_async_copy(hrecv, hrecv, halo_send_sem).wait()
     pltpu.make_async_copy(krecv, krecv, k_send_sem).wait()

time: 45.4 us -> 45 us (level)
  no operation moved by 1% of the time
where the time goes in v2:
time: 45 us; the launch traced here: 44.9 us
  Pallas kernels  43.6 us (97%)
  between operations  0.64 us (1%)
  local copies, waits for them, and re-layouts  0.62 us (1%)
    pallas_call x1, Pallas kernels, body(): pl.pallas_call(functools.partial(kernel, regions, depth_y, depth_z, fine_...  43.6 us

profile of v2, /device:TPU:1, one launch (start us, length us, event | category | flops | bytes accessed | tf_op | source)
XLA Modules:
  0.0 44.9 jit_solution(10649309227364410982)
XLA Ops:
  0.6 43.6 %shard_map.68 = f32[2,3,1024]{2,1,0:T(4,128)S(1)} custom-call(f32[3,1024]{1,0:T(4,128)} %rhs_hbm.1, f32[3,3,27,1024]{3,2,1,0:T(8,128)} %bitcast.6, s32[26,1024]{1,0:T(8,128)} %fl_hbm.1, f32[3,3,27,128]{3,2,1,0:T(8,128)} %bitcast.7, s32[26,128]{1,0:T(8,128)} %cl_hbm.1), custom_call_target="tpu_custom_call" | custom-call | tf_op jit(solution)/shard_map/pallas_call | solution.py:678
  44.3 0.6 %slice_bitcast_fusion = (f32[3,1024]{1,0:T(4,128)}, f32[3,1024]{1,0:T(4,128)}) fusion(f32[2,3,1024]{2,1,0:T(4,128)S(1)} %shard_map.68), kind=kLoop, calls=%fused_computation | loop fusion | bytes 49152 | tf_op jit(solution)/shard_map/squeeze | solution.py:742

commit v3 on v2

--- a/solution.py
+++ b/solution.py
@@ -46,11 +46,11 @@
     return jnp.where(rows_of((8, 128)) < 4, combine(accs[:3]), combine(accs[3:]))
 
 
-def coefficients(gram, shift):
+def coefficients(gram, shifts):
     def image(x):
         y = [None] * (len(x) + 1)
         for i, value in enumerate(x):
-            y[i] = value * shift if y[i] is None else y[i] + value * shift
+            y[i] = value * shifts[i] if y[i] is None else y[i] + value * shifts[i]
             y[i + 1] = value
         return y
 
@@ -81,7 +81,7 @@
     def shadow(x):
         return total([gram[0, j] * value for j, value in enumerate(x)])
 
-    one = jnp.ones_like(shift)
+    one = jnp.ones_like(shifts[0])
     resid, direction = [one], [one]
     error = []
     rho = gram[0, 0]
@@ -574,7 +574,8 @@
     largest = jnp.max(jnp.where(lane < 64, extremes, lowest), axis=1, keepdims=True)
     smallest = -jnp.max(jnp.where(lane < 64, lowest, extremes), axis=1, keepdims=True)
     largest, smallest = jnp.broadcast_to(largest, (8, 128)), jnp.broadcast_to(smallest, (8, 128))
-    centre = 0.5 * largest + 0.5 * smallest
+    middle = 0.5 * largest + 0.5 * smallest
+    centres = [middle, 0.1 * smallest, 1.3 * largest, smallest, largest, middle]
     width = 0.5 * largest - 0.5 * smallest + 0.125 * largest
     shrink = 1.0 / width
     for kind, sink in enumerate((brecv, irecv)):
@@ -585,16 +586,16 @@
             ref[j, k : k + 1, :] = field[j : j + 1, :]
 
     for ex in range(STEPS):
-        local = coarse_local(coarse) - centre * coarse
+        local = coarse_local(coarse) - centres[2 * ex] * coarse
         keep(kv, 2 * ex, coarse)
         base = coarse
         tiles_of = coarse_wait(ex)
         halo = beside(tiles_of[0, -1], tiles_of[0, 1], tiles_of[-1, 0], tiles_of[1, 0])
         coarse = (local + coarse_remote(halo)) * shrink
-        ghost = (coarse_ghost(tiles_of, mine) - centre * halo) * shrink
+        ghost = (coarse_ghost(tiles_of, mine) - centres[2 * ex] * halo) * shrink
         keep(kv, 2 * ex + 1, coarse)
         pair = (base, coarse), (halo, ghost)
-        coarse = (coarse_local(coarse) - centre * coarse + coarse_remote(ghost)) * shrink
+        coarse = (coarse_local(coarse) - centres[2 * ex + 1] * coarse + coarse_remote(ghost)) * shrink
         if ex + 1 < STEPS:
             mine = coarse_send(ex + 1, coarse)
             lift_pair(ex, *pair)
@@ -627,7 +628,7 @@
         for i in range(BASIS)
         for j in range(i, BASIS)
     }
-    weights = [weight * shrink for weight in coefficients(entries, centre * shrink)]
+    weights = [weight * shrink for weight in coefficients(entries, [centre * shrink for centre in centres])]
 
     def mix(ref):
         out = []

time: 45 us -> 45 us (level)
  no operation moved by 1% of the time
where the time goes in v3:
time: 45 us; the launch traced here: 44.9 us
  Pallas kernels  43.6 us (97%)
  between operations  0.64 us (1%)
  local copies, waits for them, and re-layouts  0.62 us (1%)
    pallas_call x1, Pallas kernels, body(): pl.pallas_call(functools.partial(kernel, regions, depth_y, depth_z, fine_...  43.6 us

profile of v3, /device:TPU:1, one launch (start us, length us, event | category | flops | bytes accessed | tf_op | source)
XLA Modules:
  0.0 44.9 jit_solution(512077562483605993)
XLA Ops:
  0.6 43.6 %shard_map.68 = f32[2,3,1024]{2,1,0:T(4,128)S(1)} custom-call(f32[3,1024]{1,0:T(4,128)} %rhs_hbm.1, f32[3,3,27,1024]{3,2,1,0:T(8,128)} %bitcast.6, s32[26,1024]{1,0:T(8,128)} %fl_hbm.1, f32[3,3,27,128]{3,2,1,0:T(8,128)} %bitcast.7, s32[26,128]{1,0:T(8,128)} %cl_hbm.1), custom_call_target="tpu_custom_call" | custom-call | tf_op jit(solution)/shard_map/pallas_call | solution.py:679
  44.3 0.6 %slice_bitcast_fusion = (f32[3,1024]{1,0:T(4,128)}, f32[3,1024]{1,0:T(4,128)}) fusion(f32[2,3,1024]{2,1,0:T(4,128)S(1)} %shard_map.68), kind=kLoop, calls=%fused_computation | loop fusion | bytes 49152 | tf_op jit(solution)/shard_map/squeeze | solution.py:743

commit v4 on v3

--- a/solution.py
+++ b/solution.py
@@ -137,17 +137,26 @@
 
     after, before, above, below = at(0, 1), at(0, -1), at(1, 0), at(-1, 0)
 
+    def block_tile(t, which):
+        columns = pl.ds(128 * t, 128)
+        return pltpu.make_async_copy(
+            fb_hbm.at[:, :, :, columns], fb.at[:, :, :, columns], load_sem.at[which]
+        )
+
+    middle_tiles = fb.at[:, :, :, pl.ds(128, fine_dev - 256)]
     loads = [
         pltpu.make_async_copy(rhs_hbm, rhs_raw, load_sem.at[4]),
-        pltpu.make_async_copy(fb_hbm, fb, load_sem.at[0]),
+        pltpu.make_async_copy(middle_tiles, middle_tiles, load_sem.at[0]),
         pltpu.make_async_copy(cb_hbm, cb_raw, load_sem.at[1]),
         pltpu.make_async_copy(cl_hbm, cl, load_sem.at[2]),
         pltpu.make_async_copy(fl_hbm, fl, load_sem.at[3]),
     ]
     loads[0].start()
-    for i in range(3):
-        for j in range(3):
-            pltpu.make_async_copy(fb_hbm.at[i, j], fb.at[i, j], load_sem.at[0]).start()
+    face_loads = [block_tile(0, 5), block_tile(tiles - 1, 6)]
+    for load in face_loads:
+        load.start()
+    for t in range(1, tiles - 1):
+        block_tile(t, 0).start()
     for load in loads[2:]:
         load.start()
 
@@ -299,7 +308,8 @@
     loads[0].wait()
     rhs[0:3, :] = rhs_raw[...]
     rhs[4:7, :] = rhs_raw[...]
-    loads[1].wait()
+    for load in face_loads:
+        load.wait()
 
     def start_tile(t, carry):
         columns = pl.ds(pl.multiple_of(t * 128, 128), 128)
@@ -330,6 +340,7 @@
     start_tile(tiles - 1, 0)
     pl.semaphore_wait(barrier, len(OFFSETS) + (n1 - 1) + (n2 - 1))
     fine_send(0, fa)
+    loads[1].wait()
     lax.fori_loop(1, tiles - 1, start_tile, 0, unroll=UNROLL)
 
     fl_tail[...] = jnp.where(rows_of((8, fine_dev)) == 2, lanes_of((8, fine_dev)), 0)
@@ -367,6 +378,15 @@
     extremes = jnp.where(lane < 64, largest, smallest)[0:1]
 
     reduce_start(0, e1, peers1, me1, extremes)
+    fine_local(fa, fc)
+
+    head, rest = slice(0, 128), slice(128, fine_dev)
+    fa[:, rest] += smooth(rhs[:, rest] - fc[:, rest], rest)
+    halves = fine_wait(0)
+    fa[:, head] += smooth(rhs[:, head] - fc[:, head] - fine_remote(halves), head)
+    fine_send(1, fa)
+    extremes = reduce_wait(0, e1, n1, jnp.maximum)
+    reduce_start(1, e2, peers2, me2, extremes)
     fine_local(fa, fc)
 
     quarter = lane >> 5
@@ -406,15 +426,6 @@
             )
     for copy in side_copies:
         copy.start()
-    head, rest = slice(0, 128), slice(128, fine_dev)
-    fa[:, rest] += smooth(rhs[:, rest] - fc[:, rest], rest)
-    halves = fine_wait(0)
-    fa[:, head] += smooth(rhs[:, head] - fc[:, head] - fine_remote(halves), head)
-    fine_send(1, fa)
-    extremes = reduce_wait(0, e1, n1, jnp.maximum)
-    reduce_start(1, e2, peers2, me2, extremes)
-    fine_local(fa, fc)
-
     def eighths(part):
         for k in (1, 2, 4):
             part = part + pltpu.roll(part, 128 - k, 1)
@@ -720,7 +731,7 @@
             pltpu.VMEM((n1, 1, 128), F32),
             pltpu.VMEM((n2, 1, 128), F32),
             pltpu.VMEM((4, 1, 128), F32),
-            pltpu.SemaphoreType.DMA((5,)),
+            pltpu.SemaphoreType.DMA((7,)),
             pltpu.SemaphoreType.DMA,
             pltpu.SemaphoreType.DMA((exchanges,)),
             pltpu.SemaphoreType.DMA,

time: 45 us -> 45.1 us (level)
  no operation moved by 1% of the time
where the time goes in v4:
time: 45.1 us; the launch traced here: 44.9 us
  Pallas kernels  43.6 us (97%)
  between operations  0.64 us (1%)
  local copies, waits for them, and re-layouts  0.62 us (1%)
    pallas_call x1, Pallas kernels, body(): pl.pallas_call(functools.partial(kernel, regions, depth_y, depth_z, fine_...  43.6 us

profile of v4, /device:TPU:1, one launch (start us, length us, event | category | flops | bytes accessed | tf_op | source)
XLA Modules:
  0.0 44.9 jit_solution(1736424943809750558)
XLA Ops:
  0.6 43.6 %shard_map.68 = f32[2,3,1024]{2,1,0:T(4,128)S(1)} custom-call(f32[3,1024]{1,0:T(4,128)} %rhs_hbm.1, f32[3,3,27,1024]{3,2,1,0:T(8,128)} %bitcast.6, s32[26,1024]{1,0:T(8,128)} %fl_hbm.1, f32[3,3,27,128]{3,2,1,0:T(8,128)} %bitcast.7, s32[26,128]{1,0:T(8,128)} %cl_hbm.1), custom_call_target="tpu_custom_call" | custom-call | tf_op jit(solution)/shard_map/pallas_call | solution.py:690
  44.3 0.6 %slice_bitcast_fusion = (f32[3,1024]{1,0:T(4,128)}, f32[3,1024]{1,0:T(4,128)}) fusion(f32[2,3,1024]{2,1,0:T(4,128)S(1)} %shard_map.68), kind=kLoop, calls=%fused_computation | loop fusion | bytes 49152 | tf_op jit(solution)/shard_map/squeeze | solution.py:754

commit v5 on v4

--- a/solution.py
+++ b/solution.py
@@ -12,7 +12,7 @@
 RELAX = 0.6
 SLOTS = 27
 PAD = 32
-UNROLL = 2
+UNROLL = 1
 MESH = pl.DeviceIdType.MESH
 OFFSETS = ((-1, -1), (-1, 1), (1, -1), (1, 1), (0, 2), (2, 0), (0, -1), (0, 1), (-1, 0), (1, 0))
 F32 = jnp.float32

time: 45.1 us -> 45.1 us (level)
  no operation moved by 1% of the time
where the time goes in v5:
time: 45.1 us; the launch traced here: 44.9 us
  Pallas kernels  43.6 us (97%)
  between operations  0.64 us (1%)
  local copies, waits for them, and re-layouts  0.62 us (1%)
    pallas_call x1, Pallas kernels, body(): pl.pallas_call(functools.partial(kernel, regions, depth_y, depth_z, fine_...  43.6 us

profile of v5, /device:TPU:1, one launch (start us, length us, event | category | flops | bytes accessed | tf_op | source)
XLA Modules:
  0.0 44.9 jit_solution(4735501076833506939)
XLA Ops:
  0.6 43.6 %shard_map.68 = f32[2,3,1024]{2,1,0:T(4,128)S(1)} custom-call(f32[3,1024]{1,0:T(4,128)} %rhs_hbm.1, f32[3,3,27,1024]{3,2,1,0:T(8,128)} %bitcast.6, s32[26,1024]{1,0:T(8,128)} %fl_hbm.1, f32[3,3,27,128]{3,2,1,0:T(8,128)} %bitcast.7, s32[26,128]{1,0:T(8,128)} %cl_hbm.1), custom_call_target="tpu_custom_call" | custom-call | tf_op jit(solution)/shard_map/pallas_call | solution.py:690
  44.3 0.6 %slice_bitcast_fusion = (f32[3,1024]{1,0:T(4,128)}, f32[3,1024]{1,0:T(4,128)}) fusion(f32[2,3,1024]{2,1,0:T(4,128)S(1)} %shard_map.68), kind=kLoop, calls=%fused_computation | loop fusion | bytes 49152 | tf_op jit(solution)/shard_map/squeeze | solution.py:754

commit v6 on v4

--- a/solution.py
+++ b/solution.py
@@ -628,11 +628,11 @@
     gram = jnp.sum(gram, axis=0, keepdims=True)
     reduce_start(2, g1, peers1, me1, gram)
     lift_pair(STEPS - 1, *pair)
+    step_images[1, :, head] += fine_remote(fine_wait(4), 2)
     gram = reduce_wait(2, g1, n1, jnp.add)
     reduce_start(3, g2, peers2, me2, gram)
     fine_local(steps, step_images.at[STEPS - 1], 2)
-    for ex in range(1, STEPS):
-        step_images[ex, :, head] += fine_remote(fine_wait(3 + ex), 2)
+    step_images[STEPS - 1, :, head] += fine_remote(fine_wait(3 + STEPS - 1), 2)
     gram = spread(reduce_wait(3, g2, n2, jnp.add))
     entries = {
         (i, j): take(gram, jnp.full((8, 128), 8 * i + j, jnp.int32))

time: 45.1 us -> 45.1 us (level)
  no operation moved by 1% of the time
where the time goes in v6:
time: 45.1 us; the launch traced here: 44.9 us
  Pallas kernels  43.6 us (97%)
  between operations  0.64 us (1%)
  local copies, waits for them, and re-layouts  0.62 us (1%)
    pallas_call x1, Pallas kernels, body(): pl.pallas_call(functools.partial(kernel, regions, depth_y, depth_z, fine_...  43.6 us

profile of v6, /device:TPU:1, one launch (start us, length us, event | category | flops | bytes accessed | tf_op | source)
XLA Modules:
  0.0 44.9 jit_solution(3971431195367469121)
XLA Ops:
  0.6 43.6 %shard_map.68 = f32[2,3,1024]{2,1,0:T(4,128)S(1)} custom-call(f32[3,1024]{1,0:T(4,128)} %rhs_hbm.1, f32[3,3,27,1024]{3,2,1,0:T(8,128)} %bitcast.6, s32[26,1024]{1,0:T(8,128)} %fl_hbm.1, f32[3,3,27,128]{3,2,1,0:T(8,128)} %bitcast.7, s32[26,128]{1,0:T(8,128)} %cl_hbm.1), custom_call_target="tpu_custom_call" | custom-call | tf_op jit(solution)/shard_map/pallas_call | solution.py:690
  44.3 0.6 %slice_bitcast_fusion = (f32[3,1024]{1,0:T(4,128)}, f32[3,1024]{1,0:T(4,128)}) fusion(f32[2,3,1024]{2,1,0:T(4,128)S(1)} %shard_map.68), kind=kLoop, calls=%fused_computation | loop fusion | bytes 49152 | tf_op jit(solution)/shard_map/squeeze | solution.py:754
